TPU v7x, 32 devices: a whole 2x2x4 slice. The times are simulated.
32 devices in a mesh: dp: 8 (over z, y), seq: 4 (over x, core).
Axes of the slice: x: 2, y: 2, z: 4, core: 2. Of those that a mesh axis runs over, the one named last changes fastest.
Arguments:
- tokens: bfloat16 [8, 2048, 768], P('dp', 'seq'), may hold values from -6 to 6
- tissue: int32 [8], P('dp'), may hold values from 0 to 15
- norm1_gain: float32 [768], replicated, may hold values from 0.5 to 1.5
- norm1_bias: float32 [768], replicated, may hold values from -3 to 3
- norm2_gain: float32 [768], replicated, may hold values from 0.5 to 1.5
- norm2_bias: float32 [768], replicated, may hold values from -3 to 3
- qkv_weight: bfloat16 [768, 2304], replicated, may hold values from -0.21875 to 0.21875
- qkv_bias: float32 [2304], replicated, may hold values from -3 to 3
- out_weight: bfloat16 [768, 768], replicated, may hold values from -0.875 to 0.875
- out_bias: float32 [768], replicated, may hold values from -3 to 3
- up_weight: bfloat16 [768, 3072], replicated, may hold values from -0.21875 to 0.21875
- up_bias: float32 [3072], replicated, may hold values from -3 to 3
- down_weight: bfloat16 [3072, 768], replicated, may hold values from -0.109375 to 0.109375
- down_bias: float32 [768], replicated, may hold values from -3 to 3
- cotangent: bfloat16 [8, 2048, 768], P('dp', 'seq'), may hold values from -6 to 6
Outputs:
- mixed: bfloat16 [8, 2048, 768], P('dp', 'seq')
- input_grad: float32 [8, 2048, 768], P('dp', 'seq')
- norm1_gain_grad: float32 [768], replicated
- norm1_bias_grad: float32 [768], replicated
- norm2_gain_grad: float32 [768], replicated
- norm2_bias_grad: float32 [768], replicated
- qkv_weight_grad: float32 [768, 2304], replicated
- qkv_bias_grad: float32 [2304], replicated
- out_weight_grad: float32 [768, 768], replicated
- out_bias_grad: float32 [768], replicated
- up_weight_grad: float32 [768, 3072], replicated
- up_bias_grad: float32 [3072], replicated
- down_weight_grad: float32 [3072, 768], replicated
- down_bias_grad: float32 [768], replicated
All inputs are finite; a program needn't handle non-finite values.
Results may differ from a plain program's by a relative error of at most 0.01.
Values may be sent and summed in bfloat16 or wider, within the bound.
A program may use at most 192 MiB of HBM per device.

v0:
```python
import math

import jax
import jax.numpy as jnp
from jax import lax
from jax.sharding import PartitionSpec as P

D = 768
H = 12
E = 64
ROT = 16
TISSUES = 16


norm_eps = 1e-05
masked_score = -1e30


def outer_sum(left_rows, right_rows):
    return lax.dot_general(
        left_rows, right_rows, (((0,), (0,)), ((), ())), preferred_element_type=jnp.float32
    )


def times_transpose(left_rows, matrix):
    return lax.dot_general(
        left_rows, matrix, (((1,), (1,)), ((), ())), preferred_element_type=jnp.float32
    )


def norm_forward(row_data, norm_gain, norm_shift):
    centred = row_data - jnp.mean(row_data, axis=-1, keepdims=True)
    inverse = lax.rsqrt(jnp.mean(centred * centred, axis=-1, keepdims=True) + norm_eps)
    normed = centred * inverse
    return (normed * norm_gain + norm_shift, normed, inverse)


def norm_backward(out_grad, normed, inverse, norm_gain):
    scaled = out_grad * norm_gain
    inner = (
        scaled
        - jnp.mean(scaled, axis=-1, keepdims=True)
        - normed * jnp.mean(scaled * normed, axis=-1, keepdims=True)
    )
    return (inner * inverse, jnp.sum(out_grad * normed, axis=0), jnp.sum(out_grad, axis=0))


def rotary_tables(places, rotary_width):
    half_width = rotary_width // 2
    frequency = 10000.0 ** (-2.0 * jnp.arange(half_width, dtype=jnp.float32) / rotary_width)
    angles = places.astype(jnp.float32)[:, None] * frequency[None, :]
    return (jnp.cos(angles), jnp.sin(angles))


def rotate(head_data, cosine, sine):
    half_width = cosine.shape[-1]
    cos_wide = cosine[None, :, None, :]
    sin_wide = sine[None, :, None, :]
    leading = head_data[..., :half_width]
    trailing = head_data[..., half_width : 2 * half_width]
    others = head_data[..., 2 * half_width :]
    return jnp.concatenate(
        [
            leading * cos_wide - trailing * sin_wide,
            trailing * cos_wide + leading * sin_wide,
            others,
        ],
        axis=-1,
    )


def body(
    tokens,
    tissue,
    norm1_gain,
    norm1_bias,
    norm2_gain,
    norm2_bias,
    qkv_weight,
    qkv_bias,
    out_weight,
    out_bias,
    up_weight,
    up_bias,
    down_weight,
    down_bias,
    cotangent,
):
    seq_count, places, model_width = tokens.shape
    row_count = seq_count * places
    seq_devices = lax.axis_size("seq")
    full_length = places * seq_devices
    device_rank = lax.axis_index("seq")
    score_scale = 1.0 / math.sqrt(E)
    inputs = tokens.astype(jnp.float32).reshape(row_count, model_width)
    labels = jnp.arange(TISSUES, dtype=jnp.int32)
    own_table = (tissue[:, None] == labels[None, :]).astype(jnp.float32)
    counts = lax.psum(jnp.sum(own_table, axis=0), "dp")
    sentences = seq_count * lax.axis_size("dp")
    sentence_weight = sentences / (TISSUES * jnp.sum(own_table * counts[None, :], axis=1))
    first_norm, first_normed, first_inverse = norm_forward(inputs, norm1_gain, norm1_bias)
    second_norm, second_normed, second_inverse = norm_forward(inputs, norm2_gain, norm2_bias)
    first_in = first_norm.astype(jnp.bfloat16)
    second_in = second_norm.astype(jnp.bfloat16)
    joint = jnp.dot(first_in, qkv_weight, preferred_element_type=jnp.float32) + qkv_bias
    joint = joint.reshape(seq_count, places, 3, H, E)
    query_places = device_rank * places + jnp.arange(places, dtype=jnp.int32)
    cosine, sine = rotary_tables(query_places, ROT)
    query = rotate(joint[:, :, 0], cosine, sine).astype(jnp.bfloat16)
    own_keys = (
        rotate(joint[:, :, 1], cosine, sine).astype(jnp.bfloat16).reshape(seq_count, places, D)
    )
    own_values = joint[:, :, 2].astype(jnp.bfloat16).reshape(seq_count, places, D)
    whole_keys, whole_values = (
        lax.all_gather(own_keys, "seq", axis=1, tiled=True),
        lax.all_gather(own_values, "seq", axis=1, tiled=True),
    )
    whole_keys = whole_keys.reshape(seq_count, full_length, H, E)
    whole_values = whole_values.reshape(seq_count, full_length, H, E)

    def block_scores(key_start, key_block):
        raw_scores = (
            jnp.einsum("sqhe,skhe->shqk", query, key_block, preferred_element_type=jnp.float32)
            * score_scale
        )
        key_places = key_start + jnp.arange(places, dtype=jnp.int32)
        allowed = key_places[None, :] <= query_places[:, None]
        return jnp.where(allowed, raw_scores, masked_score)

    def stats_step(step_index, carry):
        running_max, running_sum = carry
        key_block = lax.dynamic_slice_in_dim(whole_keys, step_index * places, places, 1)
        scores = block_scores(step_index * places, key_block)
        new_max = jnp.maximum(running_max, jnp.max(scores, axis=-1))
        running_sum = running_sum * jnp.exp(running_max - new_max) + jnp.sum(
            jnp.exp(scores - new_max[..., None]), axis=-1
        )
        return (new_max, running_sum)

    stats_init = (
        jnp.full((seq_count, H, places), masked_score, jnp.float32),
        jnp.zeros((seq_count, H, places), jnp.float32),
    )
    running_max, running_sum = lax.fori_loop(0, device_rank + 1, stats_step, stats_init)
    log_total = running_max + jnp.log(running_sum)

    def value_step(step_index, accumulated):
        key_block = lax.dynamic_slice_in_dim(whole_keys, step_index * places, places, 1)
        value_block = lax.dynamic_slice_in_dim(whole_values, step_index * places, places, 1)
        prob_low = jnp.exp(
            block_scores(step_index * places, key_block) - log_total[..., None]
        ).astype(jnp.bfloat16)
        return accumulated + jnp.einsum(
            "shqk,skhe->sqhe", prob_low, value_block, preferred_element_type=jnp.float32
        )

    attended = lax.fori_loop(
        0, device_rank + 1, value_step, jnp.zeros((seq_count, places, H, E), jnp.float32)
    )
    heads_out = attended.reshape(row_count, D).astype(jnp.bfloat16)
    attn = jnp.dot(heads_out, out_weight, preferred_element_type=jnp.float32) + out_bias
    pre = jnp.dot(second_in, up_weight, preferred_element_type=jnp.float32) + up_bias
    act = jax.nn.gelu(pre, approximate=False).astype(jnp.bfloat16)
    branch = jnp.dot(act, down_weight, preferred_element_type=jnp.float32) + down_bias
    mixed = (inputs + attn + branch).astype(jnp.bfloat16).reshape(seq_count, places, model_width)
    grad = (cotangent.astype(jnp.float32) * sentence_weight[:, None, None]).reshape(
        row_count, model_width
    )
    grad_low = grad.astype(jnp.bfloat16)
    down_weight_grad = outer_sum(act, grad_low)
    down_bias_grad = jnp.sum(grad_low.astype(jnp.float32), axis=0)
    out_weight_grad = outer_sum(heads_out, grad_low)
    act_grad = times_transpose(grad_low, down_weight)
    slope = 0.5 * (1.0 + lax.erf(pre / math.sqrt(2.0))) + pre * jnp.exp(
        -0.5 * pre * pre
    ) / math.sqrt(2.0 * math.pi)
    pre_grad = (act_grad * slope).astype(jnp.bfloat16)
    up_weight_grad = outer_sum(second_in, pre_grad)
    up_bias_grad = jnp.sum(pre_grad.astype(jnp.float32), axis=0)
    second_grad = times_transpose(pre_grad, up_weight)
    second_rows, norm2_gain_grad, norm2_bias_grad = norm_backward(
        second_grad, second_normed, second_inverse, norm2_gain
    )
    heads_grad = (
        times_transpose(grad_low, out_weight).astype(jnp.bfloat16).reshape(seq_count, places, H, E)
    )
    delta = jnp.transpose(jnp.sum(heads_grad.astype(jnp.float32) * attended, axis=-1), (0, 2, 1))
    back_keys, back_values = (
        lax.all_gather(own_keys, "seq", axis=1, tiled=True),
        lax.all_gather(own_values, "seq", axis=1, tiled=True),
    )
    back_keys = back_keys.reshape(seq_count, full_length, H, E)
    back_values = back_values.reshape(seq_count, full_length, H, E)

    def back_step(step_index, carry):
        query_grad, key_grads, value_grads = carry
        key_start = step_index * places
        key_block = lax.dynamic_slice_in_dim(back_keys, key_start, places, 1)
        value_block = lax.dynamic_slice_in_dim(back_values, key_start, places, 1)
        prob = jnp.exp(block_scores(key_start, key_block) - log_total[..., None])
        prob_low = prob.astype(jnp.bfloat16)
        prob_grad = jnp.einsum(
            "sqhe,skhe->shqk", heads_grad, value_block, preferred_element_type=jnp.float32
        )
        score_grad = (prob * (prob_grad - delta[..., None])).astype(jnp.bfloat16)
        query_grad = (
            query_grad
            + jnp.einsum(
                "shqk,skhe->sqhe", score_grad, key_block, preferred_element_type=jnp.float32
            )
            * score_scale
        )
        key_part = (
            jnp.einsum("shqk,sqhe->skhe", score_grad, query, preferred_element_type=jnp.float32)
            * score_scale
        )
        value_part = jnp.einsum(
            "shqk,sqhe->skhe", prob_low, heads_grad, preferred_element_type=jnp.float32
        )
        key_grads = lax.dynamic_update_slice_in_dim(key_grads, key_part, key_start, 1)
        value_grads = lax.dynamic_update_slice_in_dim(value_grads, value_part, key_start, 1)
        return (query_grad, key_grads, value_grads)

    back_init = (
        jnp.zeros((seq_count, places, H, E), jnp.float32),
        jnp.zeros((seq_count, full_length, H, E), jnp.float32),
        jnp.zeros((seq_count, full_length, H, E), jnp.float32),
    )
    query_grad, key_grads, value_grads = lax.fori_loop(0, device_rank + 1, back_step, back_init)
    key_terms = key_grads.reshape(seq_count, full_length, D)
    value_terms = value_grads.reshape(seq_count, full_length, D)
    key_own, value_own = (
        lax.psum_scatter(
            key_terms.astype(jnp.bfloat16), "seq", scatter_dimension=1, tiled=True
        ).astype(jnp.float32),
        lax.psum_scatter(
            value_terms.astype(jnp.bfloat16), "seq", scatter_dimension=1, tiled=True
        ).astype(jnp.float32),
    )
    query_turned = rotate(query_grad, cosine, -sine)
    key_turned = rotate(key_own.reshape(seq_count, places, H, E), cosine, -sine)
    joint_grad = jnp.stack(
        [query_turned, key_turned, value_own.reshape(seq_count, places, H, E)], axis=2
    )
    joint_grad = joint_grad.reshape(row_count, 3 * D).astype(jnp.bfloat16)
    qkv_weight_grad = outer_sum(first_in, joint_grad)
    qkv_bias_grad = jnp.sum(joint_grad.astype(jnp.float32), axis=0)
    first_grad = times_transpose(joint_grad, qkv_weight)
    first_rows, norm1_gain_grad, norm1_bias_grad = norm_backward(
        first_grad, first_normed, first_inverse, norm1_gain
    )
    input_grad = (grad + first_rows + second_rows).reshape(seq_count, places, model_width)
    (
        norm1_gain_grad,
        norm1_bias_grad,
        norm2_gain_grad,
        norm2_bias_grad,
        qkv_weight_grad,
        qkv_bias_grad,
        out_weight_grad,
        up_weight_grad,
        up_bias_grad,
        down_weight_grad,
        down_bias_grad,
    ) = lax.psum(
        (
            norm1_gain_grad,
            norm1_bias_grad,
            norm2_gain_grad,
            norm2_bias_grad,
            qkv_weight_grad,
            qkv_bias_grad,
            out_weight_grad,
            up_weight_grad,
            up_bias_grad,
            down_weight_grad,
            down_bias_grad,
        ),
        ("dp", "seq"),
    )
    return (
        mixed,
        input_grad,
        norm1_gain_grad,
        norm1_bias_grad,
        norm2_gain_grad,
        norm2_bias_grad,
        qkv_weight_grad,
        qkv_bias_grad,
        out_weight_grad,
        down_bias_grad,
        up_weight_grad,
        up_bias_grad,
        down_weight_grad,
        down_bias_grad,
    )


def solution(mesh):
    return jax.shard_map(
        body,
        mesh=mesh,
        in_specs=(
            P("dp", "seq", None),
            P("dp"),
            P(),
            P(),
            P(),
            P(),
            P(),
            P(),
            P(),
            P(),
            P(),
            P(),
            P(),
            P(),
            P("dp", "seq", None),
        ),
        out_specs=(
            P("dp", "seq", None),
            P("dp", "seq", None),
            P(),
            P(),
            P(),
            P(),
            P(),
            P(),
            P(),
            P(),
            P(),
            P(),
            P(),
            P(),
        ),
        check_vma=False,
    )
```

profile of v0, /device:TPU:0, one launch (start us, length us, event | category | flops | bytes accessed | tf_op | source)
XLA Modules:
  0.0 825.1 jit_solution(6122219814934236619)
XLA Ops:
  10.3 5.5 convolution_add_fusion
  15.8 6.0 copy.42
  43.8 23.3 %psum.84 = f32[16]{0:T(128)S(1)} all-reduce(f32[16]{0:T(128)S(1)} %compare_convert_fusion), channel_id=1, replica_groups=mesh['dp'=8,'seq'=4] {'dp'}, use_global_device_ids=true, to_apply=%region_8.0 | all-reduce | flops 16 | bytes 128 | tf_op jit(solution)/shard_map/psum | solution.py:98
  75.2 10.0 %while.39 = (s32[]{:T(128)}, f32[1,12,512]{2,1,0:T(8,128)}, f32[1,12,512]{2,1,0:T(8,128)}, s32[]{:T(128)}, bf16[1,2048,12,64]{1,3,2,0:T(8,128)(2,1)}, /*index=5*...) while((s32[]{:T(128)}, f32[1,12,512]{2,1,0:T(8,128)}, ...), condition=%wide.region_5.0_spmd.clone, body=%wide.region_2.5_spmd.clone.sunk | while | flops 424948736 | bytes 27951308 | solution.py:144
  86.5 8.2 all-gather.3.cloned.1.call-done
  96.0 9.4 %while.40 = (s32[]{:T(128)}, f32[1,512,12,64]{1,3,2,0:T(8,128)}, s32[]{:T(128)}, bf16[1,2048,12,64]{1,3,2,0:T(8,128)(2,1)}, bf16[1,2048,12,64]{1,3,2,0:T(8,128)(...) while((s32[]{:T(128)}, f32[1,512,12,64]{1,3,2,0:T(8,128)}, ...), condition=%wide.region_7.8_spmd.clone, body=%wide.region_6.0_spmd.clone.sunk | while | flops 818545664 | bytes 7382195 | solution.py:157
  97.0 8.5 %bitcast_add_fusion.7 = f32[1,512,12,64]{1,3,2,0:T(8,128)} fusion(f32[1,512,12,64]{1,3,2,0:T(8,128)} %get-tuple-element.606, f32[12,512]{1,0:T(8,128)} %bitcast.318, pred[512,512]{1,0:T(8,128)(4,1)} %broadcast_compare_fusion.7, bf16[512,12,64]{2,1,0:T(8,128)(2,1)} %bitcast.314, bf16[1,2048,12,64]{1,3,2,0:T(8,128)(2,1)} %get-tuple-element.621, ...), kind=kOutput, calls=%fused_computation.23.clone.1 | convolution fusion | flops 818282496 | bytes 7111680 | tf_op jit(solution)/shard_map/while/body/shqk,skhe->sqhe/dot_general | solution.py:153
  114.9 29.4 %while.41 = (s32[]{:T(128)}, f32[1,512,12,64]{1,3,2,0:T(8,128)}, bf16[1,2048,12,64]{1,3,2,0:T(8,128)(2,1)}, bf16[1,2048,12,64]{1,3,2,0:T(8,128)(2,1)}, s32[]{:T(...) while((s32[]{:T(128)}, f32[1,512,12,64]{1,3,2,0:T(8,128)}, ...), condition=%wide.region_12.13_spmd.clone, body=%wide.region_11.12_spmd.clone.sunk | while | flops 2046166016 | bytes 138699280 | solution.py:229
  115.1 7.8 fusion.188
  123.2 7.4 fusion.189
  135.6 7.1 bitcast_dynamic-update-slice_fusion.5
  145.4 18.6 %fusion.63 = (bf16[512,3072]{1,0:T(8,128)(2,1)S(1)}, f32[512,3072]{1,0:T(8,128)S(1)}) fusion(f32[3072]{0:T(1024)} %param.32, bf16[768,3072]{1,0:T(8,128)(2,1)} %param.31, bf16[1,512,768]{2,1,0:T(8,128)(2,1)} %param.21, f32[768]{0:T(1024)S(1)} %copy-done.30, f32[768]{0:T(1024)S(1)} %copy-done.25, f32[512]{0:T(512)S(1)} %copy-done.32, f32[512]{0:T(512)S(1)} %copy-done.27), kind=kOutput, calls=%fused_computation.69 | convolution fusion | flops 2522087424 | bytes 14964736 | tf_op jit(solution)/shard_map/dot_general | solution.py:162
  169.3 6.9 convert_reduce_fusion
  176.2 5.6 fusion.132
  186.2 126.9 %reduce-scatter.3.cloned.1.call-done = bf16[1,512,768]{1,2,0:T(8,128)(2,1)} async-done(((bf16[1,2048,768]{1,2,0:T(8,128)(2,1)}), bf16[1,512,768]{1,2,0:T(8,128)(2,1)}) %reduce-scatter.3.cloned.1.call-update) | async-done | bytes 786448 | tf_op jit(solution)/shard_map/reduce_scatter | solution.py:233
  318.1 35.6 %reduce-scatter.5.cloned.1.call-done = bf16[1,512,768]{1,2,0:T(8,128)(2,1)} async-done(((bf16[1,2048,768]{1,2,0:T(8,128)(2,1)}), bf16[1,512,768]{1,2,0:T(8,128)(2,1)}) %reduce-scatter.5.cloned.1.call-update) | async-done | bytes 786448 | tf_op jit(solution)/shard_map/reduce_scatter | solution.py:236
  357.8 5.3 fusion.117
  363.2 6.0 fusion.136
  369.3 6.5 fusion.137
  379.1 6.1 fusion.102
  387.6 43.0 %all-reduce = (f32[768]{0:T(1024)}, f32[768]{0:T(1024)}, f32[768]{0:T(1024)}, f32[768]{0:T(1024)}, f32[2304]{0:T(1024)}, /*index=5*/f32[768]{0:T(1024)S(1)}, f32[3072]{0:T(1024)}) all-reduce(f32[768]{0:T(1024)} %get-tuple-element.263, f32[768]{0:T(1024)} %get-tuple-element.268, ...), channel_id=1, replica_groups=mesh['dp'=8,'seq'=4] {'dp','seq'}, use_global_device_ids=true, to_apply=%region_20.21 | all-reduce | flops 9216 | bytes 73728 | tf_op jit(solution)/shard_map/psum | solution.py:265
  430.6 366.0 %all-reduce.4.cloned.1.call-done = (f32[768,2304]{1,0:T(8,128)}, f32[768,768]{1,0:T(8,128)}, f32[768,3072]{1,0:T(8,128)}, f32[3072,768]{1,0:T(8,128)}) async-done(((f32[768,2304]{1,0:T(8,128)}, f32[768,768]{1,0:T(8,128)}, f32[768,3072]{1,0:T(8,128)}, f32[3072,768]{1,0:T(8,128)}), (f32[768,2304]{1,0:T(8,128)}, f32[768,768]{1,0:T(8,128)}, f32[768,3072]{1,0:T(8,128)}, ...) | async-done | bytes 28311568 | tf_op jit(solution)/shard_map/psum | solution.py:265
  797.2 6.6 copy.96
  805.2 9.3 %copy.98 = f32[768,3072]{1,0:T(8,128)} copy(f32[768,3072]{1,0:T(8,128)} %get-tuple-element.715) | data formatting | bytes 18874368
  (166 shorter events, 92.6 us)
Async XLA Ops:
  7.2 66.7 %all-gather.5.cloned.1.call-start = ((), (), s32[]{:S(2)}) async-start(), calls=%async_computation.3 | async-start | bytes 3932160 | tf_op jit(solution)/shard_map/all_gather | solution.py:115
  8.7 7.0 copy-start.26
  32.6 62.1 %all-gather.3.cloned.1.call-start = ((), (), s32[]{:S(2)}) async-start(), calls=%async_computation.2 | async-start | bytes 3932160 | tf_op jit(solution)/shard_map/all_gather | solution.py:116
  35.1 278.1 %reduce-scatter.3.cloned.1.call-start = ((), (), s32[]{:S(2)}) async-start(), calls=%async_computation.4 | async-start | bytes 3932160 | tf_op jit(solution)/shard_map/reduce_scatter | solution.py:233
  115.1 8.1 copy-start.16
  115.1 8.1 copy-start.34
  115.1 8.1 copy-start.35
  123.2 7.4 copy-start.2
  135.1 7.5 copy-start.9
  144.4 209.4 %reduce-scatter.5.cloned.1.call-start = ((), (), s32[]{:S(2)}) async-start(), calls=%async_computation.5 | async-start | bytes 3932160 | tf_op jit(solution)/shard_map/reduce_scatter | solution.py:236
  144.9 651.7 %all-reduce.4.cloned.1.call-start = ((), (), s32[]{:S(2)}) async-start(), calls=%async_computation.6 | async-start | bytes 56623104 | tf_op jit(solution)/shard_map/psum | solution.py:265
  145.4 18.6 %copy-start.14 = (bf16[1,512,768]{2,1,0:T(8,128)(2,1)S(1)}, bf16[1,512,768]{2,1,0:T(8,128)(2,1)}, u32[]{:S(2)}) copy-start(bf16[1,512,768]{2,1,0:T(8,128)(2,1)} %param.35) | copy-start | bytes 2359300
  169.3 6.9 copy-start.4
  176.2 7.8 copy-start.19
  318.1 39.7 %copy-start.36 = (f32[768]{0:T(1024)S(1)}, f32[768]{0:T(1024)}, u32[]{:S(2)}) copy-start(f32[768]{0:T(1024)} %param.23) | copy-start | bytes 9220
  369.2 6.6 copy-start.6
  369.2 6.6 copy-start.20
  369.2 6.6 copy-start.39
  369.2 6.6 copy-start.42
  369.3 6.6 copy-start.43
  430.6 373.2 %copy-start.38 = (f32[768]{0:T(1024)}, f32[768]{0:T(1024)S(1)}, u32[]{:S(2)}) copy-start(f32[768]{0:T(1024)S(1)} %get-tuple-element.714) | copy-start | bytes 9220
  803.8 10.7 %slice-start = ((s8[9437184]{0:T(1024)(128)(4,1)}), s8[4194304]{0:T(1024)(128)(4,1)S(1)}, s32[]{:S(2)}) async-start(s8[9437184]{0:T(1024)(128)(4,1)} %bitcast.302), calls=%async_computation.7 | async-start | bytes 8388608
  805.2 9.3 %slice-start.1 = ((s8[9437184]{0:T(1024)(128)(4,1)}), s8[4194304]{0:T(1024)(128)(4,1)S(1)}, s32[]{:S(2)}) async-start(s8[9437184]{0:T(1024)(128)(4,1)} %bitcast.302), calls=%async_computation.8 | async-start | bytes 8388608
  805.2 9.3 %slice-start.2 = ((s8[9437184]{0:T(1024)(128)(4,1)}), s8[1048576]{0:T(1024)(128)(4,1)S(1)}, s32[]{:S(2)}) async-start(s8[9437184]{0:T(1024)(128)(4,1)} %bitcast.302), calls=%async_computation.9 | async-start | bytes 2097152
  (29 other events, 100.9 us)
Sparse Core Ops, SparseCore 0:
  32.7 31.2 all-gather.4
  66.1 28.5 all-gather.2
  144.5 168.6 reduce-scatter.2
  315.7 37.9 reduce-scatter.4
  363.3 433.2 all-reduce.3
where the time goes:
time: 831 us; the launch traced here: 825 us
  waiting for transfers between devices  537 us (65%)
  matrix products  112 us (13%)
  blocking collectives  66.3 us (8%)
  local copies, waits for them, and re-layouts  61.4 us (7%)
  other arithmetic  31.5 us (4%)
  between operations  15.8 us (2%)
    psum x1, waiting for transfers between devices, body(): lax.psum((norm1_gain_grad, norm1_bias_grad, norm2_gain_grad, norm2_bias_g...  366 us
    reduce_scatter x1, waiting for transfers between devices, body(): lax.psum_scatter(key_terms.astype(jnp.bfloat16), 'seq', scatter_dimension...  127 us
    psum x1, blocking collectives, body(): lax.psum((norm1_gain_grad, norm1_bias_grad, norm2_gain_grad, norm2_bias_g...  43 us
    reduce_scatter x1, waiting for transfers between devices, body(): lax.psum_scatter(value_terms.astype(jnp.bfloat16), 'seq', scatter_dimensi...  35.6 us
    unnamed x80, local copies, waits for them, and re-layouts  28.7 us
    psum x1, blocking collectives, body(): counts = lax.psum(jnp.sum(own_table, axis=0), 'dp')  23.3 us
    dot_general x4, matrix products, times_transpose(): lax.dot_general(left_rows, matrix, (((1,), (1,)), ((), ())), preferred_el...  22.8 us
    dot_general x1, matrix products, body(): jnp.dot(second_in, up_weight, preferred_element_type=jnp.float32) + up_bias  18.6 us
  transfers between devices with their start and end apart: 5, of which 4 were waited for; matrix products, arithmetic and copies ran while one was open for 12% of the time, Pallas kernels for 0%

commit v1 on v0

v1 whole, which is shorter than its diff:
```python
import functools
import math

import jax
import jax.numpy as jnp
from jax import lax
from jax.experimental import pallas as pl
from jax.experimental.pallas import tpu as pltpu
from jax.sharding import PartitionSpec as P

H = 12
E = 64
ROT = 16
TISSUES = 16
norm_eps = 1e-05
masked_score = -1e30
f32 = jnp.float32
bf16 = jnp.bfloat16
MESH = pl.DeviceIdType.MESH
ANY = pl.BlockSpec(memory_space=pl.ANY)
VMEM = pl.BlockSpec(memory_space=pltpu.VMEM)
VECTOR_ROWS = 16
CORE, CHIP = 1, 2


def bits_of(count):
    return count.bit_length() - 1


def flip(index, bit):
    return index + bit - 2 * bit * (lax.div(index, bit) % 2)


def bit_at(index, bit):
    return lax.div(index, bit) % 2


class Links:
    def __init__(self, dp_count, send_sems, recv_sems):
        self.dp = lax.axis_index("dp")
        self.seq = lax.axis_index("seq")
        self.dp_bits = [1 << j for j in range(bits_of(dp_count))]
        self.send_sems, self.recv_sems, self.used = send_sems, recv_sems, 0

    def over(self, axis, bit):
        if axis == "seq":
            return (self.dp, flip(self.seq, bit))
        return (flip(self.dp, bit), self.seq)

    def barrier(self):
        semaphore = pltpu.get_barrier_semaphore()
        partners = [self.over("seq", CORE), self.over("seq", CHIP)]
        partners += [self.over("dp", bit) for bit in self.dp_bits]
        for partner in partners:
            pl.semaphore_signal(semaphore, inc=1, device_id=partner, device_id_type=MESH)
        pl.semaphore_wait(semaphore, len(partners))

    def send(self, source, target, partner):
        copy = pltpu.make_async_remote_copy(
            src_ref=source,
            dst_ref=target,
            send_sem=self.send_sems.at[self.used],
            recv_sem=self.recv_sems.at[self.used],
            device_id=partner,
            device_id_type=MESH,
        )
        self.used += 1
        copy.start()
        return copy


def drive(tasks):
    tasks = list(tasks)
    while tasks:
        tasks = [task for task in tasks if next(task, "done") != "done"]


def add_up_everywhere(links, steps, buffer):
    for number, (axis, bit) in enumerate(steps):
        copy = links.send(buffer.at[2 * number], buffer.at[2 * number + 1], links.over(axis, bit))
        yield
        copy.wait()
        buffer[2 * number + 2] = buffer[2 * number] + buffer[2 * number + 1]


def gather_kernel(dp_count, pieces, x_ref, c_ref, t_ref, xo_ref, co_ref, t_out, t_buf, sends, recvs, own_sem):
    links = Links(dp_count, sends, recvs)
    links.barrier()
    places = x_ref.shape[0]
    rows = places // pieces

    def block(owner, piece):
        return pl.ds(pl.multiple_of(owner * places + piece * rows, rows), rows)

    def one_piece(source, target, piece):
        mine = source.at[pl.ds(piece * rows, rows)]
        own = target.at[block(links.seq, piece)]
        across = links.send(mine, own, links.over("seq", CHIP))
        beside = links.send(mine, own, links.over("seq", CORE))
        yield
        across.wait()
        passed = target.at[block(flip(links.seq, CHIP), piece)]
        onward = links.send(passed, passed, links.over("seq", CORE))
        yield
        beside.wait()
        onward.wait()

    locals_ = []
    for number, (source, target) in enumerate(((x_ref, xo_ref), (c_ref, co_ref))):
        copy = pltpu.make_async_copy(
            source, target.at[pl.ds(pl.multiple_of(links.seq * places, places), places)], own_sem.at[number]
        )
        copy.start()
        locals_.append(copy)
    t_buf[0] = t_ref[...]
    tasks = [
        one_piece(source, target, piece)
        for source, target in ((x_ref, xo_ref), (c_ref, co_ref))
        for piece in range(pieces)
    ]
    tasks.append(add_up_everywhere(links, [("dp", bit) for bit in links.dp_bits], t_buf))
    drive(tasks)
    t_out[...] = t_buf[2 * len(links.dp_bits)]
    for copy in locals_:
        copy.wait()


def gather(dp_count, seq_count, x, c, table):
    pieces = 4
    places, width = x.shape
    copies = 3 * 2 * pieces + bits_of(dp_count)
    whole = jax.ShapeDtypeStruct((places * seq_count, width), x.dtype)
    return pl.pallas_call(
        functools.partial(gather_kernel, dp_count, pieces),
        out_shape=(whole, whole, jax.ShapeDtypeStruct(table.shape, f32)),
        in_specs=[ANY, ANY, VMEM],
        out_specs=(ANY, ANY, VMEM),
        scratch_shapes=[
            pltpu.VMEM((2 * bits_of(dp_count) + 1,) + table.shape, f32),
            pltpu.SemaphoreType.DMA((copies,)),
            pltpu.SemaphoreType.DMA((copies,)),
            pltpu.SemaphoreType.DMA((2,)),
        ],
        compiler_params=pltpu.CompilerParams(collective_id=0, has_side_effects=True),
        name="gather_sentence",
    )(x, c, table)


def dot(a, b, dims):
    return lax.dot_general(a, b, (dims, ((), ())), preferred_element_type=f32)


NN = ((1,), (0,))
NT = ((1,), (1,))


def attention_kernel(block, q_ref, k_ref, v_ref, g_ref, qt_ref, gt_ref, o_ref, dq_ref, dkt_ref, dvt_ref):
    length = q_ref.shape[1]
    dkt_ref[...] = jnp.zeros_like(dkt_ref)
    dvt_ref[...] = jnp.zeros_like(dvt_ref)
    for i in range(length // block):
        own = pl.ds(i * block, block)
        past = pl.ds(0, (i + 1) * block)
        q, g = q_ref[0, own, :], g_ref[0, own, :]
        keys, values = k_ref[0, past, :], v_ref[0, past, :]
        scores = dot(q, keys, NT)
        row = lax.broadcasted_iota(jnp.int32, scores.shape, 0) + i * block
        column = lax.broadcasted_iota(jnp.int32, scores.shape, 1)
        scores = jnp.where(column <= row, scores, masked_score)
        largest = jnp.max(scores, axis=1, keepdims=True)
        weight = jnp.exp(scores - largest)
        prob = weight * (1.0 / jnp.sum(weight, axis=1, keepdims=True))
        prob_low = prob.astype(bf16)
        attended = dot(prob_low, values, NN)
        o_ref[0, own, :] = attended.astype(bf16)
        delta = jnp.sum(attended * g.astype(f32), axis=1, keepdims=True)
        prob_grad = dot(g, values, NT)
        score_grad = (prob * (prob_grad - delta)).astype(bf16)
        dq_ref[0, own, :] = dot(score_grad, keys, NN) * (1.0 / math.sqrt(E))
        dkt_ref[0, :, past] += dot(qt_ref[0, :, own], score_grad, NN)
        dvt_ref[0, :, past] += dot(gt_ref[0, :, own], prob_low, NN)


def attention(q, k, v, g, qt, gt):
    heads, length, size = q.shape
    tall = pl.BlockSpec((1, length, size), lambda h: (h, 0, 0))
    wide = pl.BlockSpec((1, size, length), lambda h: (h, 0, 0))
    return pl.pallas_call(
        functools.partial(attention_kernel, min(256, length)),
        grid=(heads,),
        out_shape=(
            jax.ShapeDtypeStruct((heads, length, size), bf16),
            jax.ShapeDtypeStruct((heads, length, size), f32),
            jax.ShapeDtypeStruct((heads, size, length), f32),
            jax.ShapeDtypeStruct((heads, size, length), f32),
        ),
        in_specs=[tall, tall, tall, tall, wide, wide],
        out_specs=(tall, tall, wide, wide),
        compiler_params=pltpu.CompilerParams(vmem_limit_bytes=48 * 2**20),
        name="attention",
    )(q, k, v, g, qt, gt)


def sum_kernel(dp_count, orders, grads_ref, vec_ref, part_ref, full_ref, vec_out, sum_ref, *scratch):
    groups, rows, width = grads_ref.shape
    halves = scratch[: bits_of(dp_count)]
    vec_buf, core_buf, chip_buf, sends, recvs, own_sems = scratch[bits_of(dp_count) :]
    links = Links(dp_count, sends, recvs)
    links.barrier()

    def one_group(group):
        scatter, collect = orders[group]
        held, start, size = grads_ref.at[group], 0, rows
        for number, bit in enumerate(scatter):
            size //= 2
            mine = bit_at(links.dp, bit)
            keep = pl.ds(pl.multiple_of(mine * size, size), size)
            give = pl.ds(pl.multiple_of((1 - mine) * size, size), size)
            arrived = halves[number].at[group]
            copy = links.send(held.at[give], arrived, links.over("dp", bit))
            yield
            copy.wait()
            arrived[...] = (held[keep, :].astype(f32) + arrived[...].astype(f32)).astype(bf16)
            held, start = arrived, start + mine * size
        owners = [links.seq]

        def region(owner):
            return full_ref.at[owner, group, pl.ds(pl.multiple_of(start, size), size)]

        own = pltpu.make_async_copy(held, region(links.seq), own_sems.at[group])
        own.start()
        yield
        own.wait()
        for axis, bit in collect:
            partner = links.over(axis, bit)
            copies = [links.send(region(owner), region(owner), partner) for owner in owners]
            yield
            for copy in copies:
                copy.wait()
            if axis == "dp":
                start = start - bit_at(links.dp, bit) * size
                size *= 2
            else:
                owners = owners + [flip(owner, bit) for owner in owners]

    def one_part(which):
        core, chip = bit_at(links.seq, CORE), bit_at(links.seq, CHIP)
        copies = [
            links.send(part_ref.at[which, 2 * at + 1 - core], core_buf.at[which, at], links.over("seq", CORE))
            for at in range(2)
        ]
        yield
        for at in range(2):
            copies[at].wait()
            own = part_ref[which, 2 * at + core].astype(f32)
            core_buf[which, at] = (own + core_buf[which, at].astype(f32)).astype(bf16)
        copy = links.send(core_buf.at[which, 1 - chip], chip_buf.at[which], links.over("seq", CHIP))
        yield
        yield
        yield
        copy.wait()
        sum_ref[which] = core_buf[which, chip].astype(f32) + chip_buf[which].astype(f32)

    vec_buf[0] = vec_ref[...]
    vec_steps = [("seq", CORE), ("seq", CHIP)] + [("dp", bit) for bit in links.dp_bits]
    tasks = [one_part(which) for which in range(2)]
    tasks += [one_group(group) for group in range(groups)]
    tasks.append(add_up_everywhere(links, vec_steps, vec_buf))
    drive(tasks)
    vec_out[...] = vec_buf[2 * len(vec_steps)]


def orders_for(dp_count, groups):
    bits = [1 << j for j in range(bits_of(dp_count))]
    turned = bits[1:] + bits[:1]
    core, chip = ("seq", CORE), ("seq", CHIP)

    def both(scatter, chip_at):
        collect = [("dp", bit) for bit in reversed(scatter)]
        collect.insert(chip_at, chip)
        return (scatter, collect + [core])

    kinds = [
        both(bits, len(bits)),
        both(turned, len(bits)),
        both(bits, len(bits) - 1),
    ]
    return [kinds[group * 3 // groups] for group in range(groups)]


def sums(dp_count, seq_count, grads, vec, part):
    groups, rows, width = grads.shape
    _, _, places, _ = part.shape
    bits = bits_of(dp_count)
    copies = groups * (bits + bits + 2 * bits + 3) + 6 + bits + 2
    scratch = [pltpu.VMEM((groups, rows >> (j + 1), width), bf16) for j in range(bits)]
    scratch += [
        pltpu.VMEM((2 * (bits + 2) + 1,) + vec.shape, f32),
        pltpu.VMEM((2, 2, places, width), bf16),
        pltpu.VMEM((2, places, width), bf16),
        pltpu.SemaphoreType.DMA((copies,)),
        pltpu.SemaphoreType.DMA((copies,)),
        pltpu.SemaphoreType.DMA((groups,)),
    ]
    return pl.pallas_call(
        functools.partial(sum_kernel, dp_count, orders_for(dp_count, groups)),
        out_shape=(
            jax.ShapeDtypeStruct((seq_count, groups, rows, width), bf16),
            jax.ShapeDtypeStruct(vec.shape, f32),
            jax.ShapeDtypeStruct((2, places, width), f32),
        ),
        in_specs=[VMEM, VMEM, VMEM],
        out_specs=(ANY, VMEM, VMEM),
        scratch_shapes=scratch,
        compiler_params=pltpu.CompilerParams(
            collective_id=1, has_side_effects=True, vmem_limit_bytes=48 * 2**20
        ),
        name="sums",
    )(grads, vec, part)


def rotary_tables(length):
    half = ROT // 2
    frequency = 10000.0 ** (-2.0 * jnp.arange(half, dtype=f32) / ROT)
    angles = jnp.arange(length, dtype=jnp.int32).astype(f32)[:, None] * frequency[None, :]
    return jnp.cos(angles), jnp.sin(angles)


def rotate(heads, cosine, sine):
    half = cosine.shape[-1]
    a, b = heads[..., :half], heads[..., half : 2 * half]
    c, s = cosine[:, None, :], sine[:, None, :]
    return jnp.concatenate([a * c - b * s, b * c + a * s, heads[..., 2 * half :]], axis=-1)


def normalise(rows):
    centred = rows - jnp.mean(rows, axis=-1, keepdims=True)
    inverse = lax.rsqrt(jnp.mean(centred * centred, axis=-1, keepdims=True) + norm_eps)
    return centred * inverse, inverse


def body(
    tokens,
    tissue,
    norm1_gain,
    norm1_bias,
    norm2_gain,
    norm2_bias,
    qkv_weight,
    qkv_bias,
    out_weight,
    out_bias,
    up_weight,
    up_bias,
    down_weight,
    down_bias,
    cotangent,
):
    dp_count, seq_count = lax.axis_size("dp"), lax.axis_size("seq")
    rank = lax.axis_index("seq")
    _, places, width = tokens.shape
    length = places * seq_count
    heads = H // seq_count
    attn_width = heads * E
    hidden = up_weight.shape[1] // seq_count
    own_x, own_c = tokens.reshape(places, width), cotangent.reshape(places, width)

    labels = lax.broadcasted_iota(jnp.int32, (8, 128), 1)
    own_table = (labels == tissue[0]).astype(f32)
    x_all, c_all, table = gather(dp_count, seq_count, own_x, own_c, own_table)
    count = jnp.sum(table[0] * own_table[0])
    weight = dp_count / (TISSUES * count)

    q_w = lax.dynamic_slice_in_dim(
        qkv_weight.reshape(width, 3, H * E), rank * attn_width, attn_width, 2
    ).reshape(width, 3 * attn_width)
    q_b = lax.dynamic_slice_in_dim(qkv_bias.reshape(3, H * E), rank * attn_width, attn_width, 1).reshape(-1)
    o_w = lax.dynamic_slice_in_dim(out_weight, rank * attn_width, attn_width, 0)
    u_w = lax.dynamic_slice_in_dim(up_weight, rank * hidden, hidden, 1)
    u_b = lax.dynamic_slice_in_dim(up_bias, rank * hidden, hidden, 0)
    d_w = lax.dynamic_slice_in_dim(down_weight, rank * hidden, hidden, 0)

    normed, _ = normalise(x_all.astype(f32))
    first_in = (normed * norm1_gain + norm1_bias).astype(bf16)
    second_in = (normed * norm2_gain + norm2_bias).astype(bf16)
    grad_low = (c_all.astype(f32) * weight).astype(bf16)

    joint = (dot(first_in, q_w, NN) + q_b).reshape(length, 3, heads, E)
    cosine, sine = rotary_tables(length)
    query = (rotate(joint[:, 0], cosine, sine).astype(bf16) * (1.0 / math.sqrt(E))).astype(bf16)
    keys = rotate(joint[:, 1], cosine, sine).astype(bf16)
    values = joint[:, 2].astype(bf16)
    heads_grad = dot(grad_low, o_w, NT).astype(bf16).reshape(length, heads, E)

    tall = lambda a: jnp.transpose(a, (1, 0, 2))
    wide = lambda a: jnp.transpose(a, (1, 2, 0))
    heads_out, dq, dkt, dvt = attention(
        tall(query), tall(keys), tall(values), tall(heads_grad), wide(query), wide(heads_grad)
    )
    heads_out = tall(heads_out).reshape(length, attn_width)
    dq = rotate(tall(dq), cosine, -sine)
    dk = rotate(jnp.transpose(dkt, (2, 0, 1)), cosine, -sine)
    dv = jnp.transpose(dvt, (2, 0, 1))
    joint_grad = jnp.stack([dq, dk, dv], axis=1).reshape(length, 3 * attn_width).astype(bf16)

    pre = dot(second_in, u_w, NN) + u_b
    gate = 0.5 * (1.0 + lax.erf(pre * (1.0 / math.sqrt(2.0))))
    act = (pre * gate).astype(bf16)
    slope = gate + pre * jnp.exp(-0.5 * pre * pre) * (1.0 / math.sqrt(2.0 * math.pi))
    pre_grad = (dot(grad_low, d_w, NT) * slope).astype(bf16)
    second_grad = dot(pre_grad, u_w, NT)
    first_grad = dot(joint_grad, q_w, NT)

    mixed_part = dot(act, d_w, NN) + dot(heads_out, o_w, NN)
    row_part = first_grad * norm1_gain + second_grad * norm2_gain
    part = jnp.stack([mixed_part.astype(bf16), row_part.astype(bf16)]).reshape(2, seq_count, places, width)

    TN = ((0,), (0,))
    up_grad = dot(second_in, pre_grad, TN)
    down_grad = dot(act, grad_low, TN)
    qkv_grad = dot(first_in, joint_grad, TN)
    out_grad = dot(grad_low, heads_out, TN)
    grads = jnp.concatenate(
        [up_grad.astype(bf16), down_grad.astype(bf16), jnp.concatenate([qkv_grad, out_grad], axis=1).astype(bf16)]
    )
    groups = 6
    group_rows = grads.shape[0] // groups
    padded = -(-group_rows // (16 * dp_count)) * 16 * dp_count
    grads = jnp.pad(grads.reshape(groups, group_rows, width), ((0, 0), (0, padded - group_rows), (0, 0)))

    low_sum = jnp.sum(grad_low.astype(f32), axis=0) * (1.0 / seq_count)
    placed_up = lax.dynamic_update_slice_in_dim(
        jnp.zeros((seq_count * hidden,), f32), jnp.sum(pre_grad.astype(f32), axis=0), rank * hidden, 0
    ).reshape(-1, width)
    placed_qkv = lax.dynamic_update_slice_in_dim(
        jnp.zeros((3, H * E), f32),
        jnp.sum(joint_grad.astype(f32), axis=0).reshape(3, attn_width),
        rank * attn_width,
        1,
    ).reshape(-1, width)
    vec = jnp.concatenate(
        [
            jnp.sum(first_grad * normed, axis=0)[None],
            jnp.sum(first_grad, axis=0)[None],
            jnp.sum(second_grad * normed, axis=0)[None],
            jnp.sum(second_grad, axis=0)[None],
            low_sum[None],
            placed_up,
            placed_qkv,
        ]
    )
    used = vec.shape[0]
    vec = jnp.pad(vec, ((0, VECTOR_ROWS - used), (0, 0)))

    full, vec, part_sum = sums(dp_count, seq_count, grads, vec, part)

    x32 = own_x.astype(f32)
    mixed = (x32 + part_sum[0] + (out_bias + down_bias)).astype(bf16).reshape(tokens.shape)
    own_normed, own_inverse = normalise(x32)
    scaled = part_sum[1]
    rows_grad = own_inverse * (
        scaled
        - jnp.mean(scaled, axis=-1, keepdims=True)
        - own_normed * jnp.mean(scaled * own_normed, axis=-1, keepdims=True)
    )
    input_grad = (own_c.astype(f32) * weight + rows_grad).reshape(tokens.shape)

    full = full[:, :, :group_rows].reshape(seq_count, 3, width, width)
    up_total = jnp.transpose(full[:, 0], (1, 0, 2)).reshape(width, seq_count * hidden).astype(f32)
    down_total = full[:, 1].reshape(seq_count * hidden, width).astype(f32)
    mixed_block = full[:, 2]
    qkv_total = (
        jnp.transpose(mixed_block[:, :, : 3 * attn_width].reshape(seq_count, width, 3, attn_width), (1, 2, 0, 3))
        .reshape(width, 3 * H * E)
        .astype(f32)
    )
    out_total = jnp.transpose(mixed_block[:, :, 3 * attn_width :], (0, 2, 1)).reshape(H * E, width).astype(f32)
    return (
        mixed,
        input_grad,
        vec[0],
        vec[1],
        vec[2],
        vec[3],
        qkv_total,
        vec[9:12].reshape(-1),
        out_total,
        vec[4],
        up_total,
        vec[5:9].reshape(-1),
        down_total,
        vec[4],
    )


def solution(mesh):
    rows = P("dp", "seq", None)
    return jax.shard_map(
        body,
        mesh=mesh,
        in_specs=(rows, P("dp")) + (P(),) * 12 + (rows,),
        out_specs=(rows, rows) + (P(),) * 12,
        check_vma=False,
    )
```

time: 831 us -> 419 us (0.50)
  waiting for transfers between devices: 537 us -> 0 us
  Pallas kernels: 0 us -> 240 us
  blocking collectives: 66.3 us -> 0 us
  matrix products: 112 us -> 46.6 us
  other arithmetic: 31.5 us -> 51.1 us
  between operations: 15.8 us -> 3.13 us
  local copies, waits for them, and re-layouts: 61.4 us -> 70.6 us
    psum x1 -> x0, waiting for transfers between devices: 366 us -> none  [body(): lax.psum((norm1_gain_grad, norm1_bias_grad, norm2_gain_grad, norm2_bias_g...]
    pallas_call x0 -> x3, Pallas kernels: none -> 240 us  [the longest x1 152 us: sums(): pl.pallas_call(functools.partial(sum_kernel, dp_count, orders_for(dp_coun...]
    reduce_scatter x2 -> x0, waiting for transfers between devices: 163 us -> none  [the longest x1 127 us: body(): lax.psum_scatter(key_terms.astype(jnp.bfloat16), 'seq', scatter_dimension...]
    psum x2 -> x0, blocking collectives: 66.3 us -> none  [the longest x1 43 us: body(): lax.psum((norm1_gain_grad, norm1_bias_grad, norm2_gain_grad, norm2_bias_g...]
    dot_general x19 -> x12, matrix products: 112 us -> 46.6 us  [dot(): return lax.dot_general(a, b, (dims, ((), ())), preferred_element_type=f32)]
    slice x0 -> x1, other arithmetic: none -> 11.9 us  [body(): down_total = full[:, 1].reshape(seq_count * hidden, width).astype(f32)]
    convert_element_type x2 -> x5, other arithmetic: 0.01 us -> 10.4 us  [the longest x1 6.82 us: body(): down_total = full[:, 1].reshape(seq_count * hidden, width).astype(f32)]
    transpose x0 -> x6, local copies, waits for them, and re-layouts: none -> 10.2 us  [body(): tall = lambda a: jnp.transpose(a, (1, 0, 2))]
  transfers between devices with their start and end apart: 5 -> 0, of which waited for: 4 -> 0; matrix products, arithmetic and copies ran while one was open for 12% -> 0% of each run, Pallas kernels for 0% -> 0%
where the time goes in v1:
time: 419 us; the launch traced here: 412 us
  Pallas kernels  240 us (57%)
  local copies, waits for them, and re-layouts  70.6 us (17%)
  other arithmetic  51.1 us (12%)
  matrix products  46.6 us (11%)
    pallas_call x1, Pallas kernels, sums(): pl.pallas_call(functools.partial(sum_kernel, dp_count, orders_for(dp_coun...  152 us
    pallas_call x1, Pallas kernels, gather(): pl.pallas_call(functools.partial(gather_kernel, dp_count, pieces), out_sh...  54.6 us
    dot_general x12, matrix products, dot(): return lax.dot_general(a, b, (dims, ((), ())), preferred_element_type=f32)  46.6 us
    pallas_call x1, Pallas kernels, attention(): pl.pallas_call(functools.partial(attention_kernel, min(256, length)), gri...  33.5 us
    unnamed x70, local copies, waits for them, and re-layouts  28.5 us
    slice x1, other arithmetic, body(): down_total = full[:, 1].reshape(seq_count * hidden, width).astype(f32)  11.9 us
    transpose x6, local copies, waits for them, and re-layouts, body(): tall = lambda a: jnp.transpose(a, (1, 0, 2))  10.2 us
    concatenate x1, other arithmetic, body(): jnp.concatenate([up_grad.astype(bf16), down_grad.astype(bf16), jnp.concat...  9.18 us

profile of v1, /device:TPU:0, one launch (start us, length us, event | category | flops | bytes accessed | tf_op | source)
XLA Modules:
  0.0 411.7 jit_solution(5272709260674765896)
XLA Ops:
  0.7 5.8 %copy.54 = bf16[768,2304]{0,1:T(8,128)(2,1)} copy(bf16[768,2304]{1,0:T(8,128)(2,1)} %param.21) | data formatting | bytes 7077888 | tf_op args[6]
  9.2 54.6 %gather_sentence.1 = (bf16[2048,768]{1,0:T(8,128)(2,1)}, bf16[2048,768]{1,0:T(8,128)(2,1)}, f32[8,128]{1,0:T(8,128)}) custom-call(bf16[512,768]{1,0:T(8,128)(2,1)} %bitcast.87, bf16[512,768]{1,0:T(8,128)(2,1)} %bitcast.101, f32[8,128]{1,0:T(8,128)} %iota.77.t_ref), custom_call_target="tpu_custom_call" | custom-call | tf_op jit(solution)/shard_map/gather_sentence/pallas_call | solution.py:133
  65.8 4.1 convert_reduce_fusion
  86.6 3.1 convolution_convert_fusion
  91.2 33.5 %attention.1 = (bf16[3,2048,64]{2,1,0:T(8,128)(2,1)S(1)}, f32[3,2048,64]{2,1,0:T(8,128)}, f32[3,64,2048]{2,1,0:T(8,128)S(1)}, f32[3,64,2048]{2,1,0:T(8,128)}) custom-call(bf16[3,2048,64]{2,1,0:T(8,128)(2,1)} %copy.55.q_ref, bf16[3,2048,64]{2,1,0:T(8,128)(2,1)} %copy.56.k_ref, bf16[3,2048,64]{2,1,0:T(8,128)(2,1)} %copy.57.v_ref, ...), custom_call_target="tpu_custom_call" | custom-call | tf_op jit(solution)/shard_map/attention/pallas_call | solution.py:188
  128.7 3.5 fusion.34
  133.1 3.4 copy.59
  146.2 6.0 %multiply_convert_fusion = (bf16[2048,768]{1,0:T(8,128)(2,1)S(1)}, f32[2048,768]{1,0:T(8,128)S(1)}) fusion(f32[768]{0:T(1024)S(1)} %dynamic_slice.20, bf16[768,3072]{1,0:T(8,128)(2,1)} %param.25, s32[]{:T(128)S(6)} %select_n.4, bf16[2048,768]{1,0:T(8,128)(2,1)} %get-tuple-element.24, f32[768]{0:T(1024)S(1)} %copy-done.27, f32[768]{0:T(1024)S(1)} %copy-done.30, ...), kind=kOutput, calls=%fused_computation.29 | convolution fusion | flops 2434793472 | bytes 13788164 | tf_op jit(solution)/shard_map/dot_general | solution.py:150
  155.0 6.1 %convert_reduce_fusion.1 = (f32[768]{0:T(1024)S(1)}, bf16[2048,768]{1,0:T(8,128)(2,1)S(1)}) fusion(f32[2048,768]{1,0:T(8,128)S(1)} %get-tuple-element.101, f32[768]{0:T(1024)S(1)} %dynamic_slice.20, bf16[3072,768]{1,0:T(8,128)(2,1)} %param.27, s32[]{:T(128)S(6)} %select_n.4, bf16[2048,768]{1,0:T(8,128)(2,1)S(1)} %copy-done.10, f32[]{:T(128)S(6)} %div.58), kind=kOutput, calls=%fused_computation.27 | convolution fusion | flops 2441084160 | bytes 13768712 | tf_op jit(solution)/shard_map/dot_general | solution.py:150
  161.1 3.6 convolution_convert_fusion.1
  164.7 9.2 %maximum_maximum_fusion = bf16[2304,768]{0,1:T(8,128)(2,1)} fusion(bf16[768,192]{0,1:T(8,128)(2,1)S(1)} %copy-done.19, bf16[768,576]{0,1:T(8,128)(2,1)S(1)} %convolution_convert_fusion.2, bf16[768,768]{0,1:T(8,128)(2,1)S(1)} %fusion.33, bf16[768,768]{0,1:T(8,128)(2,1)S(1)} %convolution_convert_fusion.1), kind=kLoop, calls=%fused_computation.36 | loop fusion | flops 14155776 | bytes 7077888 | tf_op jit(solution)/shard_map/concatenate | solution.py:423
  173.9 5.7 %copy.61 = bf16[2304,768]{1,0:T(8,128)(2,1)} copy(bf16[2304,768]{0,1:T(8,128)(2,1)} %maximum_maximum_fusion) | data formatting | bytes 7077888 | tf_op jit(solution)/shard_map/concatenate | solution.py:423
  179.7 5.1 %fusion.35 = f32[2048,768]{1,0:T(8,128)S(1)} fusion(bf16[2048,768]{1,0:T(8,128)(2,1)} %copy-done.32, bf16[768,3072]{1,0:T(8,128)(2,1)} %param.25, s32[]{:T(128)S(6)} %select_n.4), kind=kOutput, calls=%fused_computation.70 | convolution fusion | flops 2415919104 | bytes 10616836 | tf_op jit(solution)/shard_map/dot_general | solution.py:150
  184.8 6.0 %fusion.60 = (f32[768]{0:T(1024)S(1)}, f32[768]{0:T(1024)S(1)}, bf16[2048,768]{1,0:T(8,128)(2,1)}, f32[768]{0:T(1024)S(1)}, f32[768]{0:T(1024)S(1)}) fusion(f32[2048]{0:T(1024)S(1)} %copy-done.23, f32[2048]{0:T(1024)S(1)} %broadcast_multiply_fusion, bf16[2048,768]{1,0:T(8,128)(2,1)S(1)} %copy-done.8, f32[2048,768]{1,0:T(8,128)S(1)} %fusion.35, ...), kind=kOutput, calls=%fused_computation.121 | convolution fusion | flops 1832383488 | bytes 15861760 | tf_op jit(solution)/shard_map/dot_general | solution.py:150
  191.9 4.8 %fusion.39 = f32[2048,768]{1,0:T(8,128)S(1)} fusion(bf16[2048,768]{1,0:T(8,128)(2,1)} %copy-done.31, bf16[3072,768]{1,0:T(8,128)(2,1)} %param.27, s32[]{:T(128)S(6)} %select_n.4), kind=kOutput, calls=%fused_computation.74 | convolution fusion | flops 2415919104 | bytes 10616836 | tf_op jit(solution)/shard_map/dot_general | solution.py:150
  198.7 3.2 pad_maximum_fusion.part_ref
  201.9 152.1 %sums.1 = (bf16[4,6,384,768]{3,2,1,0:T(8,128)(2,1)}, f32[16,768]{1,0:T(8,128)S(1)}, f32[2,512,768]{2,1,0:T(8,128)S(1)}) custom-call(bf16[6,384,768]{2,1,0:T(8,128)(2,1)} %bitcast.90, f32[16,768]{1,0:T(8,128)S(1)} %pad.4.vec_ref, bf16[2,4,512,768]{3,2,1,0:T(8,128)(2,1)} %pad_maximum_fusion.part_ref), custom_call_target="tpu_custom_call" | custom-call | tf_op jit(solution)/shard_map/sums/pallas_call | solution.py:305
  358.0 11.9 %fusion.61 = (bf16[4,1,768,768]{3,2,1,0:T(8,128)(2,1)}, f32[4,96,8,768]{3,2,1,0:T(8,128)}, bf16[4,1,768,768]{3,2,1,0:T(8,128)(2,1)}) fusion(bf16[4,3,768,768]{3,2,1,0:T(8,128)(2,1)} %bitcast.91), kind=kLoop, calls=%fused_computation.122 | loop fusion | flops 2359296 | bytes 33030144 | tf_op jit(solution)/shard_map/slice | solution.py:470
  369.9 6.6 %copy.68 = bf16[4,1,768,768]{2,3,0,1:T(8,128)(2,1)} copy(bf16[4,1,768,768]{3,2,1,0:T(8,128)(2,1)} %get-tuple-element.75) | data formatting | bytes 9437184
  379.5 3.4 copy.63
  382.9 8.0 %copy.65 = f32[768,2304]{1,0:T(8,128)} copy(f32[768,2304]{0,1:T(8,128)} %bitcast.86) | data formatting | bytes 14155776
  391.5 2.9 slice_convert_fusion.1
  394.4 8.9 %copy.69 = f32[4,96,8,768]{3,2,0,1:T(8,128)} copy(f32[4,96,8,768]{3,2,1,0:T(8,128)} %get-tuple-element.74) | data formatting | bytes 18874368 | tf_op jit(solution)/shard_map/convert_element_type | solution.py:469
  403.8 6.8 %bitcast_convert_fusion = f32[3072,768]{1,0:T(8,128)} fusion(bf16[4,1,768,768]{3,2,1,0:T(8,128)(2,1)} %get-tuple-element.73), kind=kLoop, calls=%fused_computation.34 | loop fusion | flops 2359296 | bytes 14155776 | tf_op jit(solution)/shard_map/convert_element_type | solution.py:470
  (134 shorter events, 50.1 us)
Async XLA Ops:
  0.6 86.0 %copy-start = (bf16[768,768]{1,0:T(8,128)(2,1)S(1)}, bf16[768,768]{1,0:T(8,128)(2,1)}, u32[]{:S(2)}) copy-start(bf16[768,768]{1,0:T(8,128)(2,1)} %param.23) | copy-start | bytes 3538948
  0.7 7.1 %copy-start.21 = (f32[2304]{0:T(1024)S(1)}, f32[2304]{0:T(1024)}, u32[]{:S(2)}) copy-start(f32[2304]{0:T(1024)} %param.22) | copy-start | bytes 27652
  7.7 63.3 %copy-start.16 = (bf16[768,3,192]{0,2,1:T(8,128)(2,1)}, bf16[768,3,192]{0,2,1:T(8,128)(2,1)S(1)}, u32[]{:S(2)}) copy-start(bf16[768,3,192]{0,2,1:T(8,128)(2,1)S(1)} %constant_dynamic-slice_fusion.1) | copy-start | bytes 2654212
  65.8 4.1 %copy-start.5 = (bf16[2048,768]{1,0:T(8,128)(2,1)S(1)}, bf16[2048,768]{1,0:T(8,128)(2,1)}, u32[]{:S(2)}) copy-start(bf16[2048,768]{1,0:T(8,128)(2,1)} %get-tuple-element.24) | copy-start | bytes 9437188
  71.1 2.3 copy-start.22
  73.4 2.2 copy-start.9
  76.6 1.9 copy-start.18
  128.7 3.5 copy-start.3
  136.5 3.9 copy-start.15
  140.4 2.7 copy-start.6
  140.4 2.7 copy-start.23
  140.4 2.7 copy-start.29
  143.1 3.1 copy-start.27
  143.1 3.1 copy-start.30
  146.2 6.0 %copy-start.10 = (bf16[2048,768]{1,0:T(8,128)(2,1)S(1)}, bf16[2048,768]{1,0:T(8,128)(2,1)}, u32[]{:S(2)}) copy-start(bf16[2048,768]{1,0:T(8,128)(2,1)} %get-tuple-element.25) | copy-start | bytes 9437188
  152.3 2.7 copy-start.31
  155.0 6.1 %copy-start.7 = (bf16[2048,768]{1,0:T(8,128)(2,1)S(1)}, bf16[2048,768]{1,0:T(8,128)(2,1)}, u32[]{:S(2)}) copy-start(bf16[2048,768]{1,0:T(8,128)(2,1)} %get-tuple-element.24) | copy-start | bytes 9437188
  161.1 3.6 copy-start.32
  161.1 3.6 copy-start.19
  179.7 5.1 %copy-start.8 = (bf16[2048,768]{1,0:T(8,128)(2,1)S(1)}, bf16[2048,768]{1,0:T(8,128)(2,1)}, u32[]{:S(2)}) copy-start(bf16[2048,768]{1,0:T(8,128)(2,1)} %get-tuple-element.24) | copy-start | bytes 9437188
  179.7 5.1 %copy-start.14 = (bf16[2048,3,3,64]{0,3,2,1:T(8,128)(2,1)S(1)}, bf16[2048,3,3,64]{0,3,2,1:T(8,128)(2,1)}, u32[]{:S(2)}) copy-start(bf16[2048,3,3,64]{0,3,2,1:T(8,128)(2,1)} %copy-done.13) | copy-start | bytes 7077892
  179.7 5.1 %copy-start.17 = (bf16[768,3,192]{0,2,1:T(8,128)(2,1)S(1)}, bf16[768,3,192]{0,2,1:T(8,128)(2,1)}, u32[]{:S(2)}) copy-start(bf16[768,3,192]{0,2,1:T(8,128)(2,1)} %copy-done.16) | copy-start | bytes 2654212
  201.9 152.2 %copy-start.4 = (bf16[1,512,768]{2,1,0:T(8,128)(2,1)S(1)}, bf16[1,512,768]{2,1,0:T(8,128)(2,1)}, u32[]{:S(2)}) copy-start(bf16[1,512,768]{2,1,0:T(8,128)(2,1)} %param.15) | copy-start | bytes 2359300
  358.0 52.7 %copy-start.20 = (f32[768]{0:T(1024)}, f32[768]{0:T(1024)S(1)}, u32[]{:S(2)}) copy-start(f32[768]{0:T(1024)S(1)} %get-tuple-element.133) | copy-start | bytes 9220
  (9 other events, 11.6 us)
